TPU v7x, 32 devices: a whole 2x2x4 slice. The times are simulated.
32 devices in a mesh: dom: 4 (over z), rows: 8 (over y, x, core).
Axes of the slice: x: 2, y: 2, z: 4, core: 2. Of those that a mesh axis runs over, the one named last changes fastest.
Arguments:
- blocks: bfloat16 [512, 6, 128, 128], P('rows'), may hold values from -0.15625 to 0.15625
- columns: int32 [512, 6], P('rows'), may hold values from 0 to 511, as said below
- counts: int32 [8], P('rows'), may hold values from 2 to 64, as said below
- start_block: float32 [512, 2, 32, 128], P('rows'), may hold values from -6 to 6
- shift_radius: float32 [8], P('dom'), parts along dimension 0, may hold values from 1 to 1.25
- shift_angle: float32 [8], P('dom'), parts along dimension 0, may hold values from -3.140625 to 3.140625
Outputs:
- solution: float32 [2048, 2, 64, 128], P(('dom', 'rows')), parts along dimension 0
There are 4 independent parts, one for each index of `dom`. A program takes and returns all parts, laid end to end along the dimension named above; an argument that names none is the same for every part. Nothing has to cross between parts.
Inputs may be any that keep to these rules, and one draw needn't show every extreme that they name: `counts`: live block-rows of each device; some device has all 64 live. `columns`: A live block-row i of device d lists first i itself, then three live block-rows of d, then two block-rows among the first 2 of devices other than d. A dead block-row lists only itself.
All inputs are finite; a program needn't handle non-finite values.
Results may differ from a plain program's by a relative error of at most 0.0038.
Values may be sent and summed in bfloat16 or wider, within the bound.
A program may use at most 128 MiB of HBM per device.

v0:
```python
import functools

import jax
import jax.numpy as jnp
from jax import lax
from jax.experimental import pallas as pl
from jax.experimental.pallas import tpu as pltpu
from jax.sharding import PartitionSpec as P

HB = 2
ITERS = 4
NEAR = 4
F32 = jnp.float32
BF16 = jnp.bfloat16


def pick_unroll(total, want):
    while total % want:
        want -= 1
    return want


def pair_counts(slots, far, n):
    far_rows = (n - 1) * HB
    far_pairs = (slots * far + far_rows) // 2
    near_pairs = (slots * NEAR + slots) // 2
    return -(-far_pairs // 8) * 8, -(-near_pairs // 8) * 8


def split(entry, width):
    if width & (width - 1):
        k = lax.div(entry, jnp.int32(width))
        return k, entry - k * width
    shift = width.bit_length() - 1
    return lax.shift_right_logical(entry, jnp.int32(shift)), entry & (width - 1)


def kernel(
    n, slots, far, nvec, shifts,
    meta, weight, blocks, start, out,
    near_w, far_w, drive, upper, lower, near_sum, far_sum,
    send_terms, heads, far_heads, terms, out_u, out_l,
    load_sem, out_sem, head_send, head_recv, term_send, term_recv,
):
    me = lax.axis_index("rows")
    near_total = slots * (NEAR - 1)
    far_total = slots * far
    far_rows = (n - 1) * HB
    far_pairs, near_pairs = pair_counts(slots, far, n)
    at_keep = 2 * (far_pairs + near_pairs)
    at_far_last = at_keep + far_pairs + near_pairs
    at_near_last = at_far_last + far_rows
    at_near_col = at_near_last + slots
    at_far_col = at_near_col + near_total
    at_count = at_far_col + far_total

    load_start = pltpu.make_async_copy(start, drive, load_sem.at[0])
    load_far = pltpu.make_async_copy(blocks.at[:, NEAR:], far_w.at[pl.ds(0, slots)], load_sem.at[1])
    load_near = pltpu.make_async_copy(blocks.at[:, :NEAR], near_w.at[pl.ds(0, slots)], load_sem.at[2])
    load_start.start()
    load_far.start()
    load_near.start()

    barrier = pltpu.get_barrier_semaphore()
    for off in range(1, n):
        pl.semaphore_signal(
            barrier, inc=1, device_id={"rows": lax.rem(me + off, n)},
            device_id_type=pl.DeviceIdType.MESH,
        )

    def rotated(values):
        pieces = []
        for s in range(shifts):
            re = values[(2 * s) * nvec:(2 * s + 1) * nvec]
            im = values[(2 * s + 1) * nvec:(2 * s + 2) * nvec]
            w_re = weight[s]
            w_im = weight[shifts + s]
            pieces.append(w_re * re - w_im * im)
            pieces.append(w_re * im + w_im * re)
        return jnp.concatenate(pieces, 0)

    def driven(k, half):
        return jnp.concatenate([drive[k, half]] * shifts, 0)

    load_start.wait()

    def begin(k, carry):
        alive = (k < meta[at_count]).astype(F32)
        drive[k] = drive[k] * alive
        upper[0, k] = rotated(driven(k, 0)).astype(BF16)
        lower[0, k] = rotated(driven(k, 1)).astype(BF16)
        return carry

    lax.fori_loop(0, slots, begin, 0, unroll=2)
    for p in range(2):
        upper[p, slots] = jnp.zeros(upper.shape[2:], upper.dtype)
    near_w[slots, 0] = jnp.zeros(near_w.shape[2:], near_w.dtype)
    far_w[slots, 0] = jnp.zeros(far_w.shape[2:], far_w.dtype)
    near_sum[0] = jnp.zeros(near_sum.shape[1:], near_sum.dtype)
    far_sum[0] = jnp.zeros(far_sum.shape[1:], far_sum.dtype)
    pl.semaphore_wait(barrier, n - 1)

    def head_copy(p, off):
        return pltpu.make_async_remote_copy(
            src_ref=lower.at[p, pl.ds(0, HB)],
            dst_ref=heads.at[p, pl.ds((n - off - 1) * HB, HB)],
            send_sem=head_send.at[off - 1],
            recv_sem=head_recv.at[p, n - off - 1],
            device_id={"rows": lax.rem(me + off, n)},
            device_id_type=pl.DeviceIdType.MESH,
        )

    def term_copy(p, off):
        return pltpu.make_async_remote_copy(
            src_ref=send_terms.at[pl.ds((off - 1) * HB, HB)],
            dst_ref=terms.at[p, pl.ds((n - off - 1) * HB, HB)],
            send_sem=term_send.at[off - 1],
            recv_sem=term_recv.at[p, n - off - 1],
            device_id={"rows": lax.rem(me + off, n)},
            device_id_type=pl.DeviceIdType.MESH,
        )

    def dot(a, b):
        return jnp.dot(a, b, preferred_element_type=F32)

    def sweep(s, last):
        p = lax.rem(s, 2)
        q = 1 - p
        for off in range(1, n):
            head_copy(p, off).start()

        zero = jnp.zeros(upper.shape[2:], F32)

        def running(first, pairs, blocks_of, weights, sums):
            step = pick_unroll(pairs, 24)
            group = pick_unroll(step, 8)

            def go(i, acc):
                for g in range(step // group):
                    found = []
                    for u in range(group):
                        j = i * step + g * group + u
                        lhs, rhs = [], []
                        for side in range(2):
                            e = meta[2 * (first + j) + side]
                            k, c = split(e, blocks_of)
                            lhs.append(upper[p, k])
                            rhs.append(weights[k, c])
                        found.append(dot(jnp.concatenate(lhs, 1), jnp.concatenate(rhs, 0)))
                    for u in range(group):
                        j = i * step + g * group + u
                        acc = acc * meta[at_keep + first + j].astype(F32) + found[u]
                        sums[j + 1] = acc.astype(sums.dtype)
                return acc

            lax.fori_loop(0, pairs // step, go, zero)

        running(0, far_pairs, far, far_w, far_sum)
        for off in range(1, n):
            for h in range(HB):
                row = (off - 1) * HB + h
                send_terms[row] = far_sum[meta[at_far_last + row]]
            term_copy(p, off).start()
        running(far_pairs, near_pairs, NEAR, near_w, near_sum)

        def bottom(k, extra):
            value = driven(k, 1) + near_sum[meta[at_near_last + k]]
            for row in range(extra):
                value = value + terms[p, row * HB + k].astype(F32)
            value = rotated(value)
            if last:
                out_l[k] = value
            else:
                lower[q, k] = value.astype(BF16)

        def bottom_step(k, carry):
            bottom(k, 0)
            return carry

        lax.fori_loop(HB, slots, bottom_step, 0, unroll=4)

        for off in range(1, n):
            head_copy(p, off).wait_recv()
        for row in range(far_rows):
            far_heads[row] = heads[p, row]

        step_top = pick_unroll(slots, 8)
        group_top = pick_unroll(step_top, 4)

        def top_step(i, carry):
            for g in range(step_top // group_top):
                found = []
                for u in range(group_top):
                    k = i * step_top + g * group_top + u
                    tiles = [lower[p, k]]
                    for c in range(NEAR - 1):
                        tiles.append(lower[p, meta[at_near_col + k * (NEAR - 1) + c]])
                    for c in range(far):
                        tiles.append(far_heads[meta[at_far_col + k * far + c]])
                    rhs = [near_w[k, c] for c in range(NEAR)] + [far_w[k, c] for c in range(far)]
                    found.append(lax.dot_general(
                        jnp.concatenate(tiles, 1), jnp.concatenate(rhs, 1),
                        (((1,), (1,)), ((), ())), preferred_element_type=F32,
                    ))
                for u in range(group_top):
                    k = i * step_top + g * group_top + u
                    alive = (k < meta[at_count]).astype(F32)
                    value = rotated(driven(k, 0) + found[u] * alive)
                    if last:
                        out_u[k] = value
                    else:
                        upper[q, k] = value.astype(BF16)
            return carry

        lax.fori_loop(0, slots // step_top, top_step, 0)
        if last:
            write_u.start()

        for off in range(1, n):
            term_copy(p, off).wait_recv()
        for k in range(HB):
            bottom(k, n - 1)
        if last:
            write_l.start()
        for off in range(1, n):
            head_copy(p, off).wait_send()
            term_copy(p, off).wait_send()

    write_u = pltpu.make_async_copy(out_u, out.at[:, 0], out_sem.at[0])
    write_l = pltpu.make_async_copy(out_l, out.at[:, 1], out_sem.at[1])
    load_far.wait()
    load_near.wait()

    def middle(s, carry):
        sweep(s, False)
        return carry

    lax.fori_loop(0, ITERS - 1, middle, 0)
    sweep(ITERS - 1, True)
    write_u.wait()
    write_l.wait()


def plan(columns, counts, me, n):
    slots, stored = columns.shape
    far = stored - NEAR
    owner = columns // slots
    within = columns - owner * slots
    rel = lax.rem(owner - me + n, n)
    far_rows = (n - 1) * HB
    far_pairs, near_pairs = pair_counts(slots, far, n)
    near_all = within[:, :NEAR].reshape(-1)
    far_col = jnp.clip((rel - 1) * HB + within, 0, far_rows - 1)[:, NEAR:].reshape(-1)
    far_total = far_col.shape[0]
    dest = jnp.concatenate([far_col, far_rows + near_all])
    here = jnp.arange(dest.shape[0], dtype=jnp.int32)
    entry = jnp.where(here < far_total, here, here - far_total)
    rows = jnp.arange(far_rows + slots, dtype=jnp.int32)
    same = dest[None, :] == dest[:, None]
    order = jnp.sum((same & (here[None, :] < here[:, None])).astype(jnp.int32), 1)
    even = 1 - (order & 1)
    is_near = (rows >= far_rows).astype(jnp.int32)
    dest_near = (dest >= far_rows).astype(jnp.int32)
    ahead_rows = is_near * far_pairs + jnp.sum(
        jnp.where((dest[None, :] < rows[:, None]) & (dest_near[None, :] == is_near[:, None]),
                  even[None, :], 0), 1)
    own_rows = jnp.sum(jnp.where(dest[None, :] == rows[:, None], even[None, :], 0), 1)
    ahead = dest_near * far_pairs + jnp.sum(
        jnp.where((dest[None, :] < dest[:, None]) & (dest_near[None, :] == dest_near[:, None]),
                  even[None, :], 0), 1)
    place = 2 * ahead + order
    pairs = far_pairs + near_pairs
    spots = jnp.arange(2 * pairs, dtype=jnp.int32)
    empty = jnp.where(spots < 2 * far_pairs, slots * far, slots * NEAR)
    listed = jnp.sum(
        jnp.where(place[None, :] == spots[:, None], entry[None, :] - empty[:, None], 0), 1
    ) + empty
    pair_ids = jnp.arange(pairs, dtype=jnp.int32)
    starts = (ahead_rows[None, :] == pair_ids[:, None]) & (own_rows[None, :] > 0)
    keep = 1 - jnp.sum(starts.astype(jnp.int32), 1)
    ends = jnp.where(own_rows > 0, ahead_rows + own_rows - is_near * far_pairs, 0)
    return jnp.concatenate(
        [listed, keep, ends, within[:, 1:NEAR].reshape(-1), far_col, counts]
    )


def body(blocks, columns, counts, start_block, shift_radius, shift_angle):
    me = lax.axis_index("rows")
    n = lax.axis_size("rows")
    slots, stored, width = blocks.shape[0], blocks.shape[1], blocks.shape[-1]
    far = stored - NEAR
    shifts = shift_radius.shape[0]
    two_nvec = start_block.shape[2]
    cols = shifts * two_nvec
    meta = plan(columns, counts, me, n)
    weight = jnp.concatenate(
        [jnp.cos(shift_angle) / shift_radius, -jnp.sin(shift_angle) / shift_radius]
    )
    far_rows = (n - 1) * HB
    far_pairs, near_pairs = pair_counts(slots, far, n)
    flops = ITERS * 4 * slots * stored * width * width * cols
    smem = pl.BlockSpec(memory_space=pltpu.SMEM)
    hbm = pl.BlockSpec(memory_space=pl.ANY)
    return pl.pallas_call(
        functools.partial(kernel, n, slots, far, two_nvec // 2, shifts),
        out_shape=jax.ShapeDtypeStruct((slots, 2, cols, width), F32),
        in_specs=[smem, smem, hbm, hbm],
        out_specs=hbm,
        scratch_shapes=[
            pltpu.VMEM((slots + 1, NEAR, width, width), BF16),
            pltpu.VMEM((slots + 1, far, width, width), BF16),
            pltpu.VMEM(start_block.shape, F32),
            pltpu.VMEM((2, slots + 1, cols, width), BF16),
            pltpu.VMEM((2, slots, cols, width), BF16),
            pltpu.VMEM((near_pairs + 1, cols, width), F32),
            pltpu.VMEM((far_pairs + 1, cols, width), BF16),
            pltpu.VMEM((far_rows, cols, width), BF16),
            pltpu.VMEM((2, far_rows, cols, width), BF16),
            pltpu.VMEM((far_rows, cols, width), BF16),
            pltpu.VMEM((2, far_rows, cols, width), BF16),
            pltpu.VMEM((slots, cols, width), F32),
            pltpu.VMEM((slots, cols, width), F32),
            pltpu.SemaphoreType.DMA((3,)),
            pltpu.SemaphoreType.DMA((2,)),
            pltpu.SemaphoreType.DMA((n - 1,)),
            pltpu.SemaphoreType.DMA((2, n - 1)),
            pltpu.SemaphoreType.DMA((n - 1,)),
            pltpu.SemaphoreType.DMA((2, n - 1)),
        ],
        compiler_params=pltpu.CompilerParams(
            collective_id=0, has_side_effects=True, vmem_limit_bytes=56 * 1024 * 1024
        ),
        cost_estimate=pl.CostEstimate(
            flops=flops, bytes_accessed=2 * blocks.size, transcendentals=0
        ),
    )(meta, weight, blocks, start_block)


def solution(mesh):
    placed = (
        P("rows", None, None, None),
        P("rows", None),
        P("rows"),
        P("rows", None, None, None),
        P("dom"),
        P("dom"),
    )
    return jax.shard_map(
        body,
        mesh=mesh,
        in_specs=placed,
        out_specs=P(("dom", "rows"), None, None, None),
        check_vma=False,
    )
```

profile of v0, /device:TPU:0, one launch (start us, length us, event | category | flops | bytes accessed | tf_op | source)
XLA Modules:
  0.0 61.5 jit_solution(18279541040228572130)
XLA Ops:
  0.7 0.7 %cosine_divide_fusion = (f32[2]{0:T(128)S(1)}, f32[2]{0:T(128)S(1)}) fusion(f32[2]{0:T(128)} %param.10, f32[2]{0:T(128)} %param.11), kind=kLoop, calls=%fused_computation.43 | loop fusion | flops 6 | bytes 32 | tf_op jit(solution)/shard_map/div | solution.py:297
  1.4 0.6 pad_maximum_fusion.weight
  2.0 0.7 %multiply_subtract_fusion = (s32[64,6]{0,1:T(8,128)S(1)}, s32[64,6]{0,1:T(8,128)S(1)}) fusion(s32[64,6]{0,1:T(8,128)} %param.7, s32[]{:T(128)S(6)} %axis_index.12), kind=kLoop, calls=%fused_computation.29 | loop fusion | flops 11136 | bytes 4612 | tf_op jit(solution)/shard_map/sub | solution.py:248
  2.7 0.1 copy.13
  2.8 0.1 reshape.95
  3.0 0.1 copy.12
  3.1 0.1 add.57
  3.2 0.1 copy.11
  3.3 0.1 concatenate.22
  3.4 0.2 convert_reduce_fusion
  3.7 0.2 select_reduce_fusion.2
  3.9 0.3 select_reduce_fusion.1
  4.2 0.3 select_reduce_fusion
  4.5 0.1 convert_reduce_fusion.1
  4.6 0.7 %concatenate.24.meta = s32[1095]{0:T(1024)} concatenate(s32[464]{0:T(512)S(1)} %fusion.11, s32[232]{0:T(256)S(1)} %broadcast_subtract_fusion, s32[78]{0:T(128)S(1)} %get-tuple-element.13, s32[192]{0:T(256)S(1)} %reshape.95, s32[128]{0:T(128)S(1)} %concatenate.22, s32[1]{0:T(128)S(6)} %copy.17), dimensions={0} | concatenate | bytes 8760 | tf_op jit(solution)/shard_map/concatenate | solution.py:282
  5.2 51.5 %shard_map.64 = f32[64,2,64,128]{3,2,1,0:T(8,128)} custom-call(s32[1095]{0:T(1024)} %concatenate.24.meta, f32[4]{0:T(128)} %pad_maximum_fusion.weight, bf16[64,6,128,128]{3,2,1,0:T(8,128)(2,1)} %blocks.1, f32[64,2,32,128]{3,2,1,0:T(8,128)} %start.1), custom_call_target="tpu_custom_call" | custom-call | flops 6442450944 | bytes 12582912 | tf_op jit(solution)/shard_map/pallas_call | solution.py:304
  56.7 4.8 %copy.18 = f32[64,2,64,128]{3,2,1,0:T(8,128)} copy(f32[64,2,64,128]{3,2,1,0:T(8,128)} %shard_map.64) | data formatting | bytes 8388608
  (15 shorter events, 0.1 us)
where the time goes:
time: 62.1 us; the launch traced here: 61.5 us
  Pallas kernels  51.5 us (83%)
  local copies, waits for them, and re-layouts  6.18 us (10%)
  other arithmetic  3.12 us (5%)
  between operations  0.74 us (1%)
    pallas_call x1, Pallas kernels, body(): pl.pallas_call(functools.partial(kernel, n, slots, far, two_nvec // 2, sh...  51.5 us
    unnamed x2, local copies, waits for them, and re-layouts  4.8 us

commit v1 on v0

--- a/solution.py
+++ b/solution.py
@@ -38,9 +38,9 @@
 def kernel(
     n, slots, far, nvec, shifts,
     meta, weight, blocks, start, out,
-    near_w, far_w, drive, upper, lower, near_sum, far_sum,
+    near_w, far_w, turned, drive, upper, lower, near_sum, far_sum,
     send_terms, heads, far_heads, terms, out_u, out_l,
-    load_sem, out_sem, head_send, head_recv, term_send, term_recv,
+    load_sem, far_sem, near_sem, out_sem, head_send, head_recv, term_send, term_recv,
 ):
     me = lax.axis_index("rows")
     near_total = slots * (NEAR - 1)
@@ -55,11 +55,21 @@
     at_count = at_far_col + far_total
 
     load_start = pltpu.make_async_copy(start, drive, load_sem.at[0])
-    load_far = pltpu.make_async_copy(blocks.at[:, NEAR:], far_w.at[pl.ds(0, slots)], load_sem.at[1])
-    load_near = pltpu.make_async_copy(blocks.at[:, :NEAR], near_w.at[pl.ds(0, slots)], load_sem.at[2])
+    chunk = pick_unroll(slots, 8)
+    width = turned.shape[2]
+
+    def load_far(i):
+        rows = pl.ds(i * chunk, chunk)
+        return pltpu.make_async_copy(blocks.at[rows, NEAR:], far_w.at[rows], far_sem.at[i])
+
+    def load_near(i):
+        rows = pl.ds(i * chunk, chunk)
+        return pltpu.make_async_copy(blocks.at[rows, :NEAR], near_w.at[rows], near_sem.at[i])
+
     load_start.start()
-    load_far.start()
-    load_near.start()
+    for i in range(slots // chunk):
+        load_far(i).start()
+        load_near(i).start()
 
     barrier = pltpu.get_barrier_semaphore()
     for off in range(1, n):
@@ -197,11 +207,7 @@
                         tiles.append(lower[p, meta[at_near_col + k * (NEAR - 1) + c]])
                     for c in range(far):
                         tiles.append(far_heads[meta[at_far_col + k * far + c]])
-                    rhs = [near_w[k, c] for c in range(NEAR)] + [far_w[k, c] for c in range(far)]
-                    found.append(lax.dot_general(
-                        jnp.concatenate(tiles, 1), jnp.concatenate(rhs, 1),
-                        (((1,), (1,)), ((), ())), preferred_element_type=F32,
-                    ))
+                    found.append(dot(jnp.concatenate(tiles, 1), turned[k]))
                 for u in range(group_top):
                     k = i * step_top + g * group_top + u
                     alive = (k < meta[at_count]).astype(F32)
@@ -228,8 +234,18 @@
 
     write_u = pltpu.make_async_copy(out_u, out.at[:, 0], out_sem.at[0])
     write_l = pltpu.make_async_copy(out_l, out.at[:, 1], out_sem.at[1])
-    load_far.wait()
-    load_near.wait()
+
+    def turn(i, carry):
+        load_far(i).wait()
+        load_near(i).wait()
+        for u in range(chunk):
+            k = i * chunk + u
+            for c in range(NEAR + far):
+                block = near_w[k, c] if c < NEAR else far_w[k, c - NEAR]
+                turned[k, c * width:(c + 1) * width] = block.T
+        return carry
+
+    lax.fori_loop(0, slots // chunk, turn, 0)
 
     def middle(s, carry):
         sweep(s, False)
@@ -309,6 +325,7 @@
         scratch_shapes=[
             pltpu.VMEM((slots + 1, NEAR, width, width), BF16),
             pltpu.VMEM((slots + 1, far, width, width), BF16),
+            pltpu.VMEM((slots, stored * width, width), BF16),
             pltpu.VMEM(start_block.shape, F32),
             pltpu.VMEM((2, slots + 1, cols, width), BF16),
             pltpu.VMEM((2, slots, cols, width), BF16),
@@ -320,7 +337,9 @@
             pltpu.VMEM((2, far_rows, cols, width), BF16),
             pltpu.VMEM((slots, cols, width), F32),
             pltpu.VMEM((slots, cols, width), F32),
-            pltpu.SemaphoreType.DMA((3,)),
+            pltpu.SemaphoreType.DMA((1,)),
+            pltpu.SemaphoreType.DMA((slots // pick_unroll(slots, 8),)),
+            pltpu.SemaphoreType.DMA((slots // pick_unroll(slots, 8),)),
             pltpu.SemaphoreType.DMA((2,)),
             pltpu.SemaphoreType.DMA((n - 1,)),
             pltpu.SemaphoreType.DMA((2, n - 1)),

time: 62.1 us -> 59.4 us (0.957)
  Pallas kernels: 51.5 us -> 48.7 us
    pallas_call x1, Pallas kernels: 51.5 us -> 48.7 us  [body(): pl.pallas_call(functools.partial(kernel, n, slots, far, two_nvec // 2, sh...]
where the time goes in v1:
time: 59.4 us; the launch traced here: 58.8 us
  Pallas kernels  48.7 us (82%)
  local copies, waits for them, and re-layouts  6.18 us (10%)
  other arithmetic  3.12 us (5%)
  between operations  0.74 us (1%)
    pallas_call x1, Pallas kernels, body(): pl.pallas_call(functools.partial(kernel, n, slots, far, two_nvec // 2, sh...  48.7 us
    unnamed x2, local copies, waits for them, and re-layouts  4.8 us

profile of v1, /device:TPU:0, one launch (start us, length us, event | category | flops | bytes accessed | tf_op | source)
XLA Modules:
  0.0 58.8 jit_solution(8887419283509118532)
XLA Ops:
  0.7 0.7 %cosine_divide_fusion = (f32[2]{0:T(128)S(1)}, f32[2]{0:T(128)S(1)}) fusion(f32[2]{0:T(128)} %param.10, f32[2]{0:T(128)} %param.11), kind=kLoop, calls=%fused_computation.43 | loop fusion | flops 6 | bytes 32 | tf_op jit(solution)/shard_map/div | solution.py:313
  1.4 0.6 %pad_maximum_fusion.weight = f32[4]{0:T(128)} fusion(f32[2]{0:T(128)S(1)} %get-tuple-element.12, f32[2]{0:T(128)S(1)} %get-tuple-element.11), kind=kLoop, calls=%fused_computation.41 | loop fusion | flops 4 | bytes 32 | tf_op jit(solution)/shard_map/concatenate | solution.py:312
  2.0 0.7 %multiply_subtract_fusion = (s32[64,6]{0,1:T(8,128)S(1)}, s32[64,6]{0,1:T(8,128)S(1)}) fusion(s32[64,6]{0,1:T(8,128)} %param.7, s32[]{:T(128)S(6)} %axis_index.12), kind=kLoop, calls=%fused_computation.29 | loop fusion | flops 11136 | bytes 4612 | tf_op jit(solution)/shard_map/sub | solution.py:264
  2.7 0.1 copy.13
  2.8 0.1 reshape.95
  3.0 0.1 copy.12
  3.1 0.1 add.57
  3.2 0.1 copy.11
  3.3 0.1 concatenate.22
  3.4 0.2 convert_reduce_fusion
  3.7 0.2 select_reduce_fusion.2
  3.9 0.3 select_reduce_fusion.1
  4.2 0.3 select_reduce_fusion
  4.5 0.1 convert_reduce_fusion.1
  4.6 0.7 %concatenate.24.meta = s32[1095]{0:T(1024)} concatenate(s32[464]{0:T(512)S(1)} %fusion.11, s32[232]{0:T(256)S(1)} %broadcast_subtract_fusion, s32[78]{0:T(128)S(1)} %get-tuple-element.13, s32[192]{0:T(256)S(1)} %reshape.95, s32[128]{0:T(128)S(1)} %concatenate.22, s32[1]{0:T(128)S(6)} %copy.17), dimensions={0} | concatenate | bytes 8760 | tf_op jit(solution)/shard_map/concatenate | solution.py:298
  5.2 48.7 %shard_map.64 = f32[64,2,64,128]{3,2,1,0:T(8,128)} custom-call(s32[1095]{0:T(1024)} %concatenate.24.meta, f32[4]{0:T(128)} %pad_maximum_fusion.weight, bf16[64,6,128,128]{3,2,1,0:T(8,128)(2,1)} %blocks.1, f32[64,2,32,128]{3,2,1,0:T(8,128)} %start.1), custom_call_target="tpu_custom_call" | custom-call | flops 6442450944 | bytes 12582912 | tf_op jit(solution)/shard_map/pallas_call | solution.py:320
  54.0 4.8 %copy.18 = f32[64,2,64,128]{3,2,1,0:T(8,128)} copy(f32[64,2,64,128]{3,2,1,0:T(8,128)} %shard_map.64) | data formatting | bytes 8388608
  (15 shorter events, 0.1 us)
